TPU v7x, 768 devices: a whole 4x8x12 slice. The times are simulated.
768 devices in a mesh: dp: 32 (over y, x), expert: 12 (over z), tensor: 2 (over core).
Axes of the slice: x: 4, y: 8, z: 12, core: 2. Of those that a mesh axis runs over, the one named last changes fastest.
Arguments:
- tokens: bfloat16 [98304, 2048], P(('dp', 'expert'), 'tensor'), may hold values from -6 to 6
- cotangent: bfloat16 [98304, 2048], P(('dp', 'expert'), 'tensor'), may hold values from -6 to 6
- route_ids: int32 [98304, 8], P(('dp', 'expert')), may hold values from 0 to 127, all different within a row; in each aligned block of 256 rows (0 to 255, 256 to 511, ...) at most 24 rows name the same one
- gate_codes: int32 [98304, 8], P(('dp', 'expert')), may hold values from 1 to 65535
- w_gate: bfloat16 [12, 2048, 768], P('expert', None, 'tensor'), may hold values from -0.125 to 0.125
- w_up: bfloat16 [12, 2048, 768], P('expert', None, 'tensor'), may hold values from -0.125 to 0.125
- w_down: bfloat16 [12, 2048, 768], P('expert', None, 'tensor'), may hold values from -0.21875 to 0.21875
Outputs:
- token_grad: bfloat16 [98304, 2048], P(('dp', 'expert'), 'tensor')
- grad_gate: float32 [12, 2048, 768], P('expert', 'dp', 'tensor')
- grad_up: float32 [12, 2048, 768], P('expert', 'dp', 'tensor')
- grad_down: float32 [12, 2048, 768], P('expert', 'dp', 'tensor')
Inputs may be any that keep to these rules, and one draw needn't show every extreme that they name: `route_ids`: each row names 8 different experts. Within the rows of one device (aligned blocks of 256 rows) no expert is named by more than 24 rows, and in every draw some expert is named by exactly 24 rows of some block.
All inputs are finite; a program needn't handle non-finite values.
Results may differ from a plain program's by a relative error of at most 0.02.
Values may be sent and summed in bfloat16 or wider, within the bound.
A program may use at most 64 MiB of HBM per device.

v0:
```python
import jax
import jax.numpy as jnp
from jax import lax
from jax.sharding import PartitionSpec as P

ROUTED = 128


fixed_scale = 65536.0


def slot_tables(route_ids, gate_codes, expert_count, capacity):
    token_count, route_top = route_ids.shape
    flat_ids = route_ids.reshape(-1)
    onehot = (flat_ids[:, None] == jnp.arange(expert_count, dtype=jnp.int32)[None, :]).astype(
        jnp.int32
    )
    earlier = jnp.cumsum(onehot, axis=0) - onehot
    position = jnp.sum(earlier * onehot, axis=1).reshape(token_count, route_top)
    wanted = jnp.arange(expert_count, dtype=jnp.int32)
    slot_index = jnp.arange(capacity, dtype=jnp.int32)
    matches = (route_ids[None, None, :, :] == wanted[:, None, None, None]) & (
        position[None, None, :, :] == slot_index[None, :, None, None]
    )
    placing = jnp.sum(matches.astype(jnp.float32), axis=3).astype(jnp.bfloat16)
    gate_values = gate_codes.astype(jnp.float32) / fixed_scale
    slot_gate = jnp.sum(jnp.where(matches, gate_values[None, None, :, :], 0.0), axis=(2, 3))
    return (placing, slot_gate)


def per_device(tokens, cotangent, route_ids, gate_codes, w_gate, w_up, w_down):
    token_count, route_top = route_ids.shape
    column_count = tokens.shape[1]
    local_experts = w_gate.shape[0]
    expert_devices = lax.axis_size("expert")
    total_experts = local_experts * expert_devices
    capacity = min(token_count, 3 * token_count * route_top // (2 * ROUTED))
    own_place, own_gate = slot_tables(route_ids, gate_codes, total_experts, capacity)
    moved = jnp.einsum("ect,td->ecd", own_place, tokens, preferred_element_type=jnp.float32).astype(
        jnp.bfloat16
    )
    picked = jnp.einsum("ect,td->ecd", own_place, cotangent, preferred_element_type=jnp.float32)
    scaled = (own_gate[:, :, None] * picked).astype(jnp.bfloat16)
    send_shape = (expert_devices, local_experts, capacity, column_count)
    moved, scaled = (
        lax.all_to_all(
            moved.reshape(send_shape), "expert", split_axis=0, concat_axis=2, tiled=True
        ),
        lax.all_to_all(
            scaled.reshape(send_shape), "expert", split_axis=0, concat_axis=2, tiled=True
        ),
    )
    slot_rows = expert_devices * capacity
    stacked = jnp.stack(
        [
            moved.reshape(local_experts, slot_rows, column_count),
            scaled.reshape(local_experts, slot_rows, column_count),
        ]
    )
    full_rows = lax.all_gather(stacked, "tensor", axis=3, tiled=True)
    full_moved = full_rows[0]
    full_scaled = full_rows[1]
    pre_gate = jnp.einsum("erd,edf->erf", full_moved, w_gate, preferred_element_type=jnp.float32)
    pre_up = jnp.einsum("erd,edf->erf", full_moved, w_up, preferred_element_type=jnp.float32)
    d_hidden = jnp.einsum("erd,edf->erf", full_scaled, w_down, preferred_element_type=jnp.float32)
    sigma_gate = jax.nn.sigmoid(pre_gate)
    activated = pre_gate * sigma_gate
    hidden = (activated * pre_up).astype(jnp.bfloat16)
    d_gate = (d_hidden * pre_up * sigma_gate * (1.0 + pre_gate * (1.0 - sigma_gate))).astype(
        jnp.bfloat16
    )
    d_up = (d_hidden * activated).astype(jnp.bfloat16)
    route_part = jnp.einsum("erf,edf->erd", d_gate, w_gate, preferred_element_type=jnp.float32)
    route_part = route_part + jnp.einsum(
        "erf,edf->erd", d_up, w_up, preferred_element_type=jnp.float32
    )
    weight_parts = jnp.stack(
        [
            jnp.einsum("erd,erf->edf", full_moved, d_gate, preferred_element_type=jnp.float32),
            jnp.einsum("erd,erf->edf", full_moved, d_up, preferred_element_type=jnp.float32),
            jnp.einsum("erd,erf->edf", full_scaled, hidden, preferred_element_type=jnp.float32),
        ]
    )
    route_grad = lax.psum_scatter(
        route_part.astype(jnp.bfloat16), "tensor", scatter_dimension=2, tiled=True
    )
    route_grad = route_grad.reshape(local_experts, expert_devices, capacity, column_count)
    returned = lax.all_to_all(route_grad, "expert", split_axis=1, concat_axis=1, tiled=True)
    own_blocks = own_place.reshape(expert_devices, local_experts, capacity, token_count)
    token_grad = jnp.einsum(
        "encd,nect->td", returned, own_blocks, preferred_element_type=jnp.float32
    ).astype(jnp.bfloat16)
    summed = lax.psum_scatter(
        weight_parts.astype(jnp.bfloat16), "dp", scatter_dimension=2, tiled=True
    ).astype(jnp.float32)
    return (token_grad, summed[0], summed[1], summed[2])


def solution(mesh):
    in_specs = (
        P(("dp", "expert"), "tensor"),
        P(("dp", "expert"), "tensor"),
        P(("dp", "expert"), None),
        P(("dp", "expert"), None),
        P("expert", None, "tensor"),
        P("expert", None, "tensor"),
        P("expert", None, "tensor"),
    )
    out_specs = (
        P(("dp", "expert"), "tensor"),
        P("expert", "dp", "tensor"),
        P("expert", "dp", "tensor"),
        P("expert", "dp", "tensor"),
    )
    return jax.shard_map(
        per_device, mesh=mesh, in_specs=in_specs, out_specs=out_specs, check_vma=False
    )
```

profile of v0, /device:TPU:1, one launch (start us, length us, event | category | flops | bytes accessed | tf_op | source)
XLA Modules:
  0.0 381.2 jit_solution(11432882478702390949)
XLA Ops:
  7.2 1.0 copy.24
  8.2 0.1 eq.70
  8.3 0.1 eq.66
  8.4 0.7 iota_compare_fusion.3
  9.1 3.4 reduce-window.6
  12.5 0.4 slice_reduce_fusion
  12.9 0.2 reduce-window.9
  13.1 0.1 broadcast_add_fusion
  13.5 1.4 fusion.5
  15.0 1.1 fusion.18
  16.1 15.7 %all-to-all-start.1 = ((bf16[12,1,24,1024]{3,2,1,0:T(8,128)(2,1)}), bf16[12,1,24,1024]{3,2,1,0:T(8,128)(2,1)S(1)}, u32[]{:S(2)}, u32[]{:S(2)}) async-start(bf16[12,1,24,1024]{3,2,1,0:T(8,128)(2,1)} %fusion.18), calls=%async_computation.1 | async-start | bytes 1179648 | tf_op jit(solution)/shard_map/all_to_all | solution.py:49
  31.9 0.3 fusion.19
  32.3 22.8 %all-to-all-done.1 = bf16[12,1,24,1024]{3,2,1,0:T(8,128)(2,1)S(1)} async-done(((bf16[12,1,24,1024]{3,2,1,0:T(8,128)(2,1)}), bf16[12,1,24,1024]{3,2,1,0:T(8,128)(2,1)S(1)}, u32[]{:S(2)}, u32[]{:S(2)}) %all-to-all-start.1) | async-done | bytes 589856 | tf_op jit(solution)/shard_map/all_to_all | solution.py:49
  55.1 31.1 %all_to_all.29 = bf16[12,1,24,1024]{3,2,1,0:T(8,128)(2,1)S(1)} all-to-all(bf16[12,1,24,1024]{3,2,1,0:T(8,128)(2,1)S(1)} %fusion.19), channel_id=1, replica_groups=mesh['dp'=32,'expert'=12,'tensor'=2] {'expert'}, dimensions={0} | all-to-all | bytes 1179648 | tf_op jit(solution)/shard_map/all_to_all | solution.py:46
  86.2 1.1 pad_maximum_fusion.1
  87.4 20.7 %all-gather.2.cloned.1.call-done = bf16[2,1,288,2048]{3,2,1,0:T(8,128)(2,1)} async-done(((bf16[2,1,288,1024]{3,2,1,0:T(8,128)(2,1)}), bf16[2,1,288,2048]{3,2,1,0:T(8,128)(2,1)}) %all-gather.2.cloned.1.call-update) | async-done | bytes 2359312 | tf_op jit(solution)/shard_map/all_gather | solution.py:60
  108.1 2.2 fusion.9
  110.3 0.8 fusion.12
  111.2 0.8 copy-done.8
  111.9 0.8 multiply_convert_fusion.1
  112.8 0.8 fusion.7
  113.6 1.9 fusion.4
  115.5 2.6 fusion.2
  118.2 1.2 fusion.1
  119.4 1.2 fusion.3
  120.6 2.5 pad_maximum_fusion
  123.1 13.4 %reduce-scatter.3.cloned.1.call-done = bf16[1,288,1024]{2,1,0:T(8,128)(2,1)} async-done(((bf16[1,288,2048]{2,1,0:T(8,128)(2,1)}), bf16[1,288,1024]{2,1,0:T(8,128)(2,1)}) %reduce-scatter.3.cloned.1.call-update) | async-done | bytes 589840 | tf_op jit(solution)/shard_map/reduce_scatter | solution.py:84
  136.5 33.4 %all_to_all.30 = bf16[1,12,24,1024]{3,2,0,1:T(8,128)(2,1)S(1)} all-to-all(bf16[1,12,24,1024]{3,2,0,1:T(8,128)(2,1)} %bitcast.86), channel_id=1, replica_groups=mesh['dp'=32,'expert'=12,'tensor'=2] {'expert'}, dimensions={1} | all-to-all | bytes 1179648 | tf_op jit(solution)/shard_map/all_to_all | solution.py:88
  169.9 1.3 fusion.17
  171.2 201.8 %reduce-scatter.5.cloned.1.call-done = bf16[3,1,64,384]{3,2,1,0:T(8,128)(2,1)} async-done(((bf16[3,1,2048,384]{3,2,1,0:T(8,128)(2,1)}), bf16[3,1,64,384]{3,2,1,0:T(8,128)(2,1)}) %reduce-scatter.5.cloned.1.call-update) | async-done | bytes 147472 | tf_op jit(solution)/shard_map/reduce_scatter | solution.py:93
  373.0 0.9 convert_element_type.70
  374.0 0.7 slice_bitcast_fusion.8
  (39 shorter events, 0.5 us)
Async XLA Ops:
  7.2 100.9 %copy-start = (bf16[1,2048,384]{2,1,0:T(8,128)(2,1)S(1)}, bf16[1,2048,384]{2,1,0:T(8,128)(2,1)}, u32[]{:S(2)}) copy-start(bf16[1,2048,384]{2,1,0:T(8,128)(2,1)} %param.11) | copy-start | bytes 4718596
  7.2 6.3 %copy-start.5 = (s32[256,8]{0,1:T(8,128)S(1)}, s32[256,8]{0,1:T(8,128)}, u32[]{:S(2)}) copy-start(s32[256,8]{0,1:T(8,128)} %param.10) | copy-start | bytes 24580
  7.2 7.8 %copy-start.2 = (bf16[256,1024]{1,0:T(8,128)(2,1)S(1)}, bf16[256,1024]{1,0:T(8,128)(2,1)}, u32[]{:S(2)}) copy-start(bf16[256,1024]{1,0:T(8,128)(2,1)} %param.8) | copy-start | bytes 1572868
  13.3 18.7 %copy-start.3 = (bf16[256,1024]{1,0:T(8,128)(2,1)S(1)}, bf16[256,1024]{1,0:T(8,128)(2,1)}, u32[]{:S(2)}) copy-start(bf16[256,1024]{1,0:T(8,128)(2,1)} %param.7) | copy-start | bytes 1572868
  16.1 38.9 %all-to-all-start.1 = ((bf16[12,1,24,1024]{3,2,1,0:T(8,128)(2,1)}), bf16[12,1,24,1024]{3,2,1,0:T(8,128)(2,1)S(1)}, u32[]{:S(2)}, u32[]{:S(2)}) async-start(bf16[12,1,24,1024]{3,2,1,0:T(8,128)(2,1)} %fusion.18), calls=%async_computation.1 | async-start | bytes 1179648 | tf_op jit(solution)/shard_map/all_to_all | solution.py:49
  31.9 76.2 %all-gather.2.cloned.1.call-start = ((), (), s32[]{:S(2)}) async-start(), calls=%async_computation.5 | async-start | bytes 3538944 | tf_op jit(solution)/shard_map/all_gather | solution.py:60
  87.3 23.0 %copy-start.1 = (bf16[1,2048,384]{2,1,0:T(8,128)(2,1)S(1)}, bf16[1,2048,384]{2,1,0:T(8,128)(2,1)}, u32[]{:S(2)}) copy-start(bf16[1,2048,384]{2,1,0:T(8,128)(2,1)} %param.12) | copy-start | bytes 4718596
  87.3 49.2 %reduce-scatter.3.cloned.1.call-start = ((), (), s32[]{:S(2)}) async-start(), calls=%async_computation.6 | async-start | bytes 1769472 | tf_op jit(solution)/shard_map/reduce_scatter | solution.py:84
  108.1 2.2 copy-start.6
  110.3 0.8 copy-start.9
  110.3 1.6 copy-start.8
  111.9 0.8 copy-start.11
  112.8 0.8 copy-start.4
  115.5 257.5 %reduce-scatter.5.cloned.1.call-start = ((), (), s32[]{:S(2)}) async-start(), calls=%async_computation.7 | async-start | bytes 4866048 | tf_op jit(solution)/shard_map/reduce_scatter | solution.py:93
  115.5 2.6 copy-start.7
  118.2 1.2 copy-start.10
  118.2 1.2 copy-start.12
Sparse Core Ops, SparseCore 0:
  87.4 20.6 all-gather.1
  115.6 20.8 reduce-scatter.2
  142.4 230.5 reduce-scatter.4
where the time goes:
time: 385 us; the launch traced here: 381 us
  waiting for transfers between devices  259 us (67%)
  blocking collectives  64.5 us (17%)
  starting transfers between devices  15.8 us (4%)
  matrix products  14.2 us (4%)
  between operations  14.1 us (4%)
  other arithmetic  10.5 us (3%)
    reduce_scatter x1, waiting for transfers between devices, per_device(): lax.psum_scatter(weight_parts.astype(jnp.bfloat16), 'dp', scatter_dimensi...  202 us
    all_to_all x1, blocking collectives, per_device(): lax.all_to_all(route_grad, 'expert', split_axis=1, concat_axis=1, tiled=T...  33.4 us
    all_to_all x1, blocking collectives, per_device(): lax.all_to_all(moved.reshape(send_shape), 'expert', split_axis=0, concat_...  31.1 us
    all_to_all x1, waiting for transfers between devices, per_device(): lax.all_to_all(scaled.reshape(send_shape), 'expert', split_axis=0, concat...  22.8 us
    all_gather x1, waiting for transfers between devices, per_device(): full_rows = lax.all_gather(stacked, 'tensor', axis=3, tiled=True)  20.7 us
    all_to_all x1, starting transfers between devices, per_device(): lax.all_to_all(scaled.reshape(send_shape), 'expert', split_axis=0, concat...  15.7 us
    reduce_scatter x1, waiting for transfers between devices, per_device(): lax.psum_scatter(route_part.astype(jnp.bfloat16), 'tensor', scatter_dimen...  13.4 us
  transfers between devices with their start and end apart: 4, of which 4 were waited for; matrix products, arithmetic and copies ran while one was open for 2% of the time, Pallas kernels for 0%

commit v1 on v0

v1 whole, which is shorter than its diff:
```python
import functools

import jax
import jax.numpy as jnp
from jax import lax
from jax.experimental import pallas as pl
from jax.experimental.pallas import tpu as pltpu
from jax.sharding import PartitionSpec as P

MESH = pl.DeviceIdType.MESH
F32 = jnp.float32
BF16 = jnp.bfloat16
NX, NY, NZ = 4, 8, 12
CAP = 24
SLOTS = NZ * CAP
GATE_UNIT = 65536.0


def chains_of(n):
    half = n // 2
    listed, slot = [], 0
    for sign, part, length in ((1, 0, half), (-1, 1, half), (1, 1, half - 1), (-1, 0, half - 1)):
        listed.append((sign, part, length, slot))
        slot += length
    return listed


def kernel(
    ids_ref, codes_ref, tok_hbm, cot_hbm, wg_hbm, wu_hbm, wd_hbm,
    out_tok, out_gate, out_up, out_down,
    tok, cot, wg, wu, wd, place, send_x, send_c, recv_x, recv_c, x_full, c_full, pre_gate, pre_up,
    d_both, hidden, own_part, peer_out, peer_in, back_out, back_in,
    pa, pb, pa2, pb2, ra, rb, ra2, rb2,
    in_sem, zx_s, zx_r, zc_s, zc_r, tx_s, tx_r, tc_s, tc_r, loc_sem, p_s, p_r, back_s, back_r,
    ra_s, ra_r, rb_s, rb_r, ra2_s, ra2_r, rb2_s, rb2_r,
):
    dp = lax.axis_index("dp")
    z = lax.axis_index("expert")
    c = lax.axis_index("tensor")
    y, x = dp // NX, dp % NX
    peer = 1 - c
    cols = tok.shape[1]

    loads = [
        pltpu.make_async_copy(src, dst, in_sem.at[i])
        for i, (src, dst) in enumerate(((tok_hbm, tok), (cot_hbm, cot), (wg_hbm, wg), (wu_hbm, wu), (wd_hbm, wd)))
    ]
    for load in loads:
        load.start()

    def at_z(k):
        return (dp, k, c)

    def at_x(k):
        return (y * NX + k, z, c)

    def at_y(k):
        return (k * NX + x, z, c)

    at_peer = (dp, z, peer)

    barrier = pltpu.get_barrier_semaphore()

    def greet(i, carry):
        pl.semaphore_signal(barrier, inc=1, device_id=at_z(lax.rem(z + i, NZ)), device_id_type=MESH)
        return carry

    lax.fori_loop(1, NZ, greet, 0)
    pl.semaphore_signal(barrier, inc=1, device_id=at_peer, device_id_type=MESH)
    for step in (1, NX - 1):
        pl.semaphore_signal(barrier, inc=1, device_id=at_x(lax.rem(x + step, NX)), device_id_type=MESH)
    for step in (1, NY - 1):
        pl.semaphore_signal(barrier, inc=1, device_id=at_y(lax.rem(y + step, NY)), device_id_type=MESH)

    count = ids_ref.shape[1]
    expert_row = lax.broadcasted_iota(jnp.int32, (16, count), 0)
    match = jnp.zeros((16, count), F32)
    gates = jnp.zeros((16, count), F32)
    for k in range(ids_ref.shape[0]):
        same = ids_ref[k : k + 1, :] == expert_row
        match = match + jnp.where(same, 1.0, 0.0)
        gates = gates + jnp.where(same, codes_ref[k : k + 1, :].astype(F32) / GATE_UNIT, 0.0)
    before = jnp.where(
        lax.broadcasted_iota(jnp.int32, (count, count), 0) < lax.broadcasted_iota(jnp.int32, (count, count), 1),
        1.0, 0.0,
    ).astype(BF16)
    position = jnp.dot(match.astype(BF16), before, preferred_element_type=F32)
    position = jnp.where(match > 0.5, position, -1.0)
    slot_row = lax.broadcasted_iota(jnp.int32, (CAP, count), 0).astype(F32)
    pieces, slot_gates = [], []
    for e in range(NZ):
        piece = jnp.where(position[e : e + 1, :] == slot_row, 1.0, 0.0)
        pieces.append(piece)
        slot_gates.append(jnp.sum(piece * gates[e : e + 1, :], axis=1, keepdims=True))
    place[...] = jnp.concatenate(pieces, axis=0).astype(BF16)
    slot_gate = jnp.concatenate(slot_gates, axis=0)

    def z_copy(src, dst, send, recv, target, slab):
        return pltpu.make_async_remote_copy(
            src_ref=src.at[target], dst_ref=dst.at[c, slab], send_sem=send.at[target], recv_sem=recv.at[slab],
            device_id=at_z(target), device_id_type=MESH,
        )

    def t_copy(src, dst, half, send, recv, slab):
        return pltpu.make_async_remote_copy(
            src_ref=src, dst_ref=dst.at[half, slab], send_sem=send.at[slab], recv_sem=recv.at[slab],
            device_id=at_peer, device_id_type=MESH,
        )

    def turn(i):
        step = (i + 1) // 2
        return lax.rem(z + NZ + jnp.where(i % 2 == 1, step, -step), NZ)

    def gather(table, buffer, scale):
        for block in range(cols // 256):
            part = jnp.dot(place[...], table[:, block * 256 : block * 256 + 256], preferred_element_type=F32)
            if scale is not None:
                part = scale * part
            for e in range(NZ):
                buffer[e, :, block * 256 : block * 256 + 256] = part[e * CAP : (e + 1) * CAP, :].astype(BF16)

    def send_all(src, dst, zs, zr, ts, tr, own):
        def one(i, carry):
            z_copy(src, dst, zs, zr, turn(i), z).start()
            return carry

        lax.fori_loop(1, NZ, one, 0)
        t_copy(src.at[z], dst, c, ts, tr, z).start()
        own_copy = pltpu.make_async_copy(src.at[z], dst.at[c, z], loc_sem.at[own])
        own_copy.start()
        return own_copy

    loads[0].wait()
    gather(tok, send_x, None)
    pl.semaphore_wait(barrier, NZ - 1 + 5)
    own_x = send_all(send_x, recv_x, zx_s, zx_r, tx_s, tx_r, 0)
    loads[1].wait()
    gather(cot, send_c, slot_gate)
    own_c = send_all(send_c, recv_c, zc_s, zc_r, tc_s, tc_r, 1)

    def pass_on(src, dst, zs, zr, ts, tr):
        def one(i, carry):
            slab = turn(i)
            z_copy(src, dst, zs, zr, slab, slab).wait_recv()
            t_copy(dst.at[c, slab], dst, c, ts, tr, slab).start()
            return carry

        lax.fori_loop(1, NZ, one, 0)

    def from_peer(src, dst, ts, tr):
        def one(i, carry):
            t_copy(src.at[i], dst, peer, ts, tr, i).wait_recv()
            return carry

        lax.fori_loop(0, NZ, one, 0)

    def assemble(slabs, full):
        for half in range(2):
            def one(b, carry, half=half):
                col = pl.multiple_of(b * 256, 256)
                rows = [slabs[half, e, :, pl.ds(col, 256)].astype(F32) for e in range(NZ)]
                full[:, pl.ds(pl.multiple_of(half * cols + b * 256, 256), 256)] = jnp.concatenate(rows, axis=0).astype(BF16)
                return carry

            lax.fori_loop(0, cols // 256, one, 0)

    pass_on(send_x, recv_x, zx_s, zx_r, tx_s, tx_r)
    own_x.wait()
    from_peer(send_x, recv_x, tx_s, tx_r)
    assemble(recv_x, x_full)
    loads[2].wait()
    loads[3].wait()
    pre_gate[...] = jnp.dot(x_full[...], wg[...], preferred_element_type=F32)
    pre_up[...] = jnp.dot(x_full[...], wu[...], preferred_element_type=F32)
    loads[4].wait()

    pass_on(send_c, recv_c, zc_s, zc_r, tc_s, tc_r)
    own_c.wait()
    from_peer(send_c, recv_c, tc_s, tc_r)
    assemble(recv_c, c_full)
    d_hidden = jnp.dot(c_full[...], wd[...], preferred_element_type=F32)
    sigma = jax.nn.sigmoid(pre_gate[...])
    activated = pre_gate[...] * sigma
    width = hidden.shape[1]
    hidden[...] = (activated * pre_up[...]).astype(BF16)
    d_both[:, :width] = (
        d_hidden * pre_up[...] * sigma * (1.0 + pre_gate[...] * (1.0 - sigma))
    ).astype(BF16)
    d_both[:, width:] = (d_hidden * activated).astype(BF16)

    over_rows = (((0,), (0,)), ((), ()))

    def weight_block(b, carry):
        col = pl.multiple_of(b * 256, 256)
        both = lax.dot_general(x_full[:, pl.ds(col, 256)], d_both[...], over_rows, preferred_element_type=F32)
        down = lax.dot_general(c_full[:, pl.ds(col, 256)], hidden[...], over_rows, preferred_element_type=F32)
        for m, value in enumerate((both[:, :width], both[:, width:], down)):
            value = value.astype(BF16)
            for k in range(NX):
                for q in range(4):
                    rows = value[k * 64 + q * 16 : k * 64 + q * 16 + 16, :]
                    if q < 2:
                        pa[b, q, k, m * 16 : m * 16 + 16, :] = rows
                    else:
                        pb[k, q - 2, b, m * 16 : m * 16 + 16, :] = rows
        return carry

    lax.fori_loop(0, NY, weight_block, 0)

    rings = {
        "a": (NY, y, at_y, pa, ra, ra_s, ra_r),
        "b": (NX, x, at_x, pb, rb, rb_s, rb_r),
        "a2": (NX, x, at_x, pa2, ra2, ra2_s, ra2_r),
        "b2": (NY, y, at_y, pb2, rb2, rb2_s, rb2_r),
    }

    def hop(ring, chain, h):
        n, me, at, parts, slots, send, recv = rings[ring]
        sign, part, length, base = chain
        target = lax.rem(me + n + sign, n)
        dest = lax.rem(me + n + sign * (length - h), n)
        src = parts.at[dest, part] if h == 0 else slots.at[base + h - 1]
        return pltpu.make_async_remote_copy(
            src_ref=src, dst_ref=slots.at[base + h], send_sem=send.at[base + h], recv_sem=recv.at[base + h],
            device_id=at(target), device_id_type=MESH,
        )

    def begin(ring):
        for chain in chains_of(rings[ring][0]):
            hop(ring, chain, 0).start()

    def serve(ring, which, h):
        n, me, at, parts, slots, send, recv = rings[ring]
        for chain in chains_of(n)[2 * which : 2 * which + 2]:
            sign, part, length, base = chain
            hop(ring, chain, h).wait_recv()
            if h < length - 1:
                dest = lax.rem(me + n + sign * (length - h - 1), n)

                def add(i, carry, base=base, h=h, dest=dest, part=part):
                    total = slots[base + h, i].astype(F32) + parts[dest, part, i].astype(F32)
                    slots[base + h, i] = total.astype(BF16)
                    return carry

                lax.fori_loop(0, parts.shape[2], add, 0)
                hop(ring, chain, h + 1).start()

    def finish(ring, store):
        n, me, at, parts, slots, send, recv = rings[ring]
        for part in range(2):
            last = [base + length - 1 for sign, p, length, base in chains_of(n) if p == part]

            def one(i, carry, part=part, last=last):
                store(
                    part, i,
                    parts[me, part, i].astype(F32) + slots[last[0], i].astype(F32) + slots[last[1], i].astype(F32),
                )
                return carry

            lax.fori_loop(0, parts.shape[2], one, 0)

    def to_a2(part, i, total):
        pa2[i, part, 0] = total.astype(BF16)

    def to_b2(part, i, total):
        pb2[i, part, 0] = total.astype(BF16)

    def to_out(first):
        def store(part, i, total):
            row = (first + part) * 16
            for m, out in enumerate((out_gate, out_up, out_down)):
                out[row : row + 16, :] = total[m * 16 : m * 16 + 16, :]

        return store

    begin("a")
    begin("b")

    over_width = (((1,), (1,)), ((), ()))

    def route_block(row):
        rows = pl.ds(pl.multiple_of(row, 256), 256)
        return lax.dot_general(
            d_both[:, :width], wg[rows, :], over_width, preferred_element_type=F32
        ) + lax.dot_general(d_both[:, width:], wu[rows, :], over_width, preferred_element_type=F32)

    def peer_copy(b):
        return pltpu.make_async_remote_copy(
            src_ref=peer_out.at[b], dst_ref=peer_in.at[b], send_sem=p_s.at[b], recv_sem=p_r.at[b],
            device_id=at_peer, device_id_type=MESH,
        )

    blocks = cols // 256

    def for_peer(b, carry):
        peer_out[b] = route_block(peer * cols + b * 256).astype(BF16)
        peer_copy(b).start()
        return carry

    def for_own(b, carry):
        own_part[b] = route_block(c * cols + b * 256)
        return carry

    lax.fori_loop(0, blocks, for_peer, 0)
    lax.fori_loop(0, blocks, for_own, 0)
    serve("a", 0, 0)

    def join(b, carry):
        peer_copy(b).wait_recv()
        total = (own_part[b] + peer_in[b].astype(F32))
        col = pl.multiple_of(b * 256, 256)
        for e in range(NZ):
            back_out[e, :, pl.ds(col, 256)] = total[e * CAP : (e + 1) * CAP, :].astype(BF16)
        return carry

    lax.fori_loop(0, blocks, join, 0)

    def back_copy(target, slab):
        return pltpu.make_async_remote_copy(
            src_ref=back_out.at[target], dst_ref=back_in.at[slab], send_sem=back_s.at[target],
            recv_sem=back_r.at[slab], device_id=at_z(target), device_id_type=MESH,
        )

    def send_back(i, carry):
        back_copy(turn(i), z).start()
        return carry

    lax.fori_loop(1, NZ, send_back, 0)
    own_back = pltpu.make_async_copy(back_out.at[z], back_in.at[z], loc_sem.at[2])
    own_back.start()

    serve("a", 1, 0)
    serve("b", 0, 0)
    serve("a", 0, 1)
    serve("a", 1, 1)
    serve("b", 1, 0)
    serve("a", 0, 2)
    serve("a", 1, 2)
    serve("b", 0, 1)
    finish("b", to_b2)
    begin("b2")
    serve("a", 0, 3)
    finish("a", to_a2)
    begin("a2")
    serve("b2", 0, 0)
    serve("b2", 1, 0)
    serve("a2", 0, 0)
    serve("a2", 1, 0)
    serve("b2", 0, 1)
    serve("b2", 1, 1)
    serve("a2", 0, 1)
    finish("a2", to_out(0))
    serve("b2", 0, 2)
    serve("b2", 1, 2)
    serve("b2", 0, 3)
    finish("b2", to_out(2))

    def arrived(i, carry):
        back_copy(turn(i), turn(i)).wait_recv()
        return carry

    lax.fori_loop(1, NZ, arrived, 0)
    own_back.wait()

    def token_block(b, carry):
        col = pl.multiple_of(b * 256, 256)
        rows = [back_in[e, :, pl.ds(col, 256)].astype(F32) for e in range(NZ)]
        rows = jnp.concatenate(rows, axis=0).astype(BF16)
        out_tok[:, pl.ds(col, 256)] = lax.dot_general(
            place[...], rows, over_rows, preferred_element_type=F32
        ).astype(BF16)
        return carry

    lax.fori_loop(0, blocks, token_block, 0)

    def sent(i, carry):
        target = turn(i)
        z_copy(send_x, recv_x, zx_s, zx_r, target, z).wait_send()
        z_copy(send_c, recv_c, zc_s, zc_r, target, z).wait_send()
        back_copy(target, z).wait_send()
        return carry

    lax.fori_loop(1, NZ, sent, 0)

    def sent_peer(i, carry):
        t_copy(send_x.at[i], recv_x, c, tx_s, tx_r, i).wait_send()
        t_copy(send_c.at[i], recv_c, c, tc_s, tc_r, i).wait_send()
        return carry

    lax.fori_loop(0, NZ, sent_peer, 0)

    def sent_blocks(b, carry):
        peer_copy(b).wait_send()
        return carry

    lax.fori_loop(0, blocks, sent_blocks, 0)
    for ring in rings:
        for chain in chains_of(rings[ring][0]):
            for h in range(chain[2]):
                hop(ring, chain, h).wait_send()


def per_device(tokens, cotangent, route_ids, gate_codes, w_gate, w_up, w_down):
    rows, cols = tokens.shape
    depth, width = w_gate.shape[1:]
    dma = lambda n: pltpu.SemaphoreType.DMA((n,))
    vm = pltpu.VMEM
    a_hops, b_hops = NY - 1, NX - 1
    scratch = [
        vm((rows, cols), BF16), vm((rows, cols), BF16),
        vm((depth, width), BF16), vm((depth, width), BF16), vm((depth, width), BF16),
        vm((SLOTS, rows), BF16),
        vm((NZ, CAP, cols), BF16), vm((NZ, CAP, cols), BF16),
        vm((2, NZ, CAP, cols), BF16), vm((2, NZ, CAP, cols), BF16),
        vm((SLOTS, depth), BF16), vm((SLOTS, depth), BF16),
        vm((SLOTS, width), F32), vm((SLOTS, width), F32),
        vm((SLOTS, 2 * width), BF16), vm((SLOTS, width), BF16),
        vm((cols // 256, SLOTS, 256), F32), vm((cols // 256, SLOTS, 256), BF16), vm((cols // 256, SLOTS, 256), BF16),
        vm((NZ, CAP, cols), BF16), vm((NZ, CAP, cols), BF16),
        vm((NY, 2, NX, 48, width), BF16), vm((NX, 2, NY, 48, width), BF16),
        vm((NX, 2, 1, 48, width), BF16), vm((NY, 2, 1, 48, width), BF16),
        vm((2 * a_hops, NX, 48, width), BF16), vm((2 * b_hops, NY, 48, width), BF16),
        vm((2 * b_hops, 1, 48, width), BF16), vm((2 * a_hops, 1, 48, width), BF16),
        dma(5), dma(NZ), dma(NZ), dma(NZ), dma(NZ), dma(NZ), dma(NZ), dma(NZ), dma(NZ), dma(3),
        dma(4), dma(4), dma(NZ), dma(NZ),
        dma(2 * a_hops), dma(2 * a_hops), dma(2 * b_hops), dma(2 * b_hops),
        dma(2 * b_hops), dma(2 * b_hops), dma(2 * a_hops), dma(2 * a_hops),
    ]
    in_vmem = pl.BlockSpec(memory_space=pltpu.VMEM)
    anywhere = pl.BlockSpec(memory_space=pl.ANY)
    out_rows = depth // (NX * NY)
    weight_out = jax.ShapeDtypeStruct((out_rows, width), F32)
    token_grad, grad_gate, grad_up, grad_down = pl.pallas_call(
        kernel,
        out_shape=(jax.ShapeDtypeStruct((rows, cols), BF16), weight_out, weight_out, weight_out),
        in_specs=[in_vmem, in_vmem] + [anywhere] * 5,
        out_specs=(in_vmem,) * 4,
        scratch_shapes=scratch,
        compiler_params=pltpu.CompilerParams(
            collective_id=0, has_side_effects=True, vmem_limit_bytes=56 * 1024 * 1024
        ),
        name="moe_backward",
    )(route_ids.T, gate_codes.T, tokens, cotangent, w_gate[0], w_up[0], w_down[0])
    return token_grad, grad_gate[None], grad_up[None], grad_down[None]


def solution(mesh):
    in_specs = (
        P(("dp", "expert"), "tensor"),
        P(("dp", "expert"), "tensor"),
        P(("dp", "expert"), None),
        P(("dp", "expert"), None),
        P("expert", None, "tensor"),
        P("expert", None, "tensor"),
        P("expert", None, "tensor"),
    )
    out_specs = (
        P(("dp", "expert"), "tensor"),
        P("expert", "dp", "tensor"),
        P("expert", "dp", "tensor"),
        P("expert", "dp", "tensor"),
    )
    return jax.shard_map(
        per_device, mesh=mesh, in_specs=in_specs, out_specs=out_specs, check_vma=False
    )
```

time: 385 us -> 113 us (0.29)
  waiting for transfers between devices: 259 us -> 0 us
  Pallas kernels: 0 us -> 104 us
  blocking collectives: 64.5 us -> 0 us
  starting transfers between devices: 15.8 us -> 0 us
  matrix products: 14.2 us -> 0 us
  between operations: 14.1 us -> 0.64 us
  other arithmetic: 10.5 us -> 0 us
    reduce_scatter x2 -> x0, waiting for transfers between devices: 215 us -> none  [the longest x1 202 us: per_device(): lax.psum_scatter(weight_parts.astype(jnp.bfloat16), 'dp', scatter_dimensi...]
    pallas_call x0 -> x1, Pallas kernels: none -> 104 us  [per_device(): pl.pallas_call(kernel, out_shape=(jax.ShapeDtypeStruct((rows, cols), BF16...]
    all_to_all x2 -> x0, blocking collectives: 64.5 us -> none  [the longest x1 33.4 us: per_device(): lax.all_to_all(route_grad, 'expert', split_axis=1, concat_axis=1, tiled=T...]
    all_to_all x1 -> x0, waiting for transfers between devices: 22.8 us -> none  [per_device(): lax.all_to_all(scaled.reshape(send_shape), 'expert', split_axis=0, concat...]
    all_gather x1 -> x0, waiting for transfers between devices: 20.7 us -> none  [per_device(): full_rows = lax.all_gather(stacked, 'tensor', axis=3, tiled=True)]
    all_to_all x1 -> x0, starting transfers between devices: 15.7 us -> none  [per_device(): lax.all_to_all(scaled.reshape(send_shape), 'expert', split_axis=0, concat...]
    dot_general x11 -> x0, matrix products: 14.2 us -> none  [the longest x1 2.61 us: per_device(): jnp.einsum('erd,erf->edf', full_moved, d_up, preferred_element_type=jnp.f...]
    another operation x5 -> x0, other arithmetic: 7.29 us -> none
  transfers between devices with their start and end apart: 4 -> 0, of which waited for: 4 -> 0; matrix products, arithmetic and copies ran while one was open for 2% -> 0% of each run, Pallas kernels for 0% -> 0%
where the time goes in v1:
time: 113 us; the launch traced here: 111 us
  Pallas kernels  104 us (92%)
  local copies, waits for them, and re-layouts  6.48 us (6%)
    pallas_call x1, Pallas kernels, per_device(): pl.pallas_call(kernel, out_shape=(jax.ShapeDtypeStruct((rows, cols), BF16...  104 us
    unnamed x4, local copies, waits for them, and re-layouts  6.48 us

profile of v1, /device:TPU:1, one launch (start us, length us, event | category | flops | bytes accessed | tf_op | source)
XLA Modules:
  0.0 111.2 jit_solution(10614378510123605036)
XLA Ops:
  0.6 104.1 %moe_backward.1 = (bf16[256,1024]{1,0:T(8,128)(2,1)}, f32[64,384]{1,0:T(8,128)}, f32[64,384]{1,0:T(8,128)}, f32[64,384]{1,0:T(8,128)}) custom-call(s32[8,256]{1,0:T(8,128)} %bitcast.14, s32[8,256]{1,0:T(8,128)} %bitcast.15, bf16[256,1024]{1,0:T(8,128)(2,1)} %tok_hbm.1, bf16[256,1024]{1,0:T(8,128)(2,1)} %cot_hbm.1, bf16[2048,384]{1,0:T(8,128)(2,1)} %bitcast.8, ...), custom_call_target="tpu_custom_call" | custom-call | tf_op jit(solution)/shard_map/moe_backward/pallas_call | solution.py:433
  104.7 1.9 %copy.15 = bf16[256,1024]{1,0:T(8,128)(2,1)} copy(bf16[256,1024]{1,0:T(8,128)(2,1)} %get-tuple-element.16) | data formatting | bytes 1048576
  106.6 1.5 %copy.16 = f32[1,64,384]{2,1,0:T(8,128)} copy(f32[1,64,384]{2,1,0:T(8,128)} %bitcast.13) | data formatting | bytes 196608
  108.2 1.5 %copy.17 = f32[1,64,384]{2,1,0:T(8,128)} copy(f32[1,64,384]{2,1,0:T(8,128)} %bitcast.12) | data formatting | bytes 196608
  109.7 1.5 %copy.18 = f32[1,64,384]{2,1,0:T(8,128)} copy(f32[1,64,384]{2,1,0:T(8,128)} %bitcast.11) | data formatting | bytes 196608

commit v2 on v1

--- a/solution.py
+++ b/solution.py
@@ -16,21 +16,23 @@
 GATE_UNIT = 65536.0
 
 
+Y_ORDER = (4, 3, -3, 2, -2, 1, -1, 0)
+X_ORDER = (2, 1, -1, 0)
+A_UNITS = (((0, 0), (0, 1), (0, 2)), ((1, 0), (1, 1)))
+B_UNITS = (((2, 0), (2, 1), (2, 2)), ((3, 0), (3, 1), (3, 2), (1, 2)))
+
+
 def chains_of(n):
     half = n // 2
-    listed, slot = [], 0
-    for sign, part, length in ((1, 0, half), (-1, 1, half), (1, 1, half - 1), (-1, 0, half - 1)):
-        listed.append((sign, part, length, slot))
-        slot += length
-    return listed
+    return ((1, 0, half), (-1, 1, half), (1, 1, half - 1), (-1, 0, half - 1))
 
 
 def kernel(
     ids_ref, codes_ref, tok_hbm, cot_hbm, wg_hbm, wu_hbm, wd_hbm,
     out_tok, out_gate, out_up, out_down,
     tok, cot, wg, wu, wd, place, send_x, send_c, recv_x, recv_c, x_full, c_full, pre_gate, pre_up,
-    d_both, hidden, own_part, peer_out, peer_in, back_out, back_in,
-    pa, pb, pa2, pb2, ra, rb, ra2, rb2,
+    d_both, hidden, own_part, peer_out, peer_in, back_out, back_in, tok_grad,
+    parts_a, parts_b, parts_a2, parts_b2, slots_a, slots_b, slots_a2, slots_b2,
     in_sem, zx_s, zx_r, zc_s, zc_r, tx_s, tx_r, tc_s, tc_r, loc_sem, p_s, p_r, back_s, back_r,
     ra_s, ra_r, rb_s, rb_r, ra2_s, ra2_r, rb2_s, rb2_r,
 ):
@@ -154,31 +156,39 @@
 
         lax.fori_loop(0, NZ, one, 0)
 
-    def assemble(slabs, full):
-        for half in range(2):
-            def one(b, carry, half=half):
-                col = pl.multiple_of(b * 256, 256)
-                rows = [slabs[half, e, :, pl.ds(col, 256)].astype(F32) for e in range(NZ)]
-                full[:, pl.ds(pl.multiple_of(half * cols + b * 256, 256), 256)] = jnp.concatenate(rows, axis=0).astype(BF16)
-                return carry
-
-            lax.fori_loop(0, cols // 256, one, 0)
+    def assemble(slabs, full, half):
+        def one(b, carry):
+            col = pl.multiple_of(b * 256, 256)
+            rows = [slabs[half, e, :, pl.ds(col, 256)].astype(F32) for e in range(NZ)]
+            full[half, :, pl.ds(col, 256)] = jnp.concatenate(rows, axis=0).astype(BF16)
+            return carry
+
+        lax.fori_loop(0, cols // 256, one, 0)
+
+    def product(full, weights, half):
+        rows = pl.ds(pl.multiple_of(half * cols, cols), cols)
+        return jnp.dot(full[half], weights[rows, :], preferred_element_type=F32)
 
     pass_on(send_x, recv_x, zx_s, zx_r, tx_s, tx_r)
     own_x.wait()
     from_peer(send_x, recv_x, tx_s, tx_r)
-    assemble(recv_x, x_full)
     loads[2].wait()
     loads[3].wait()
-    pre_gate[...] = jnp.dot(x_full[...], wg[...], preferred_element_type=F32)
-    pre_up[...] = jnp.dot(x_full[...], wu[...], preferred_element_type=F32)
+    assemble(recv_x, x_full, 0)
+    assemble(recv_x, x_full, 1)
+    pre_gate[...] = product(x_full, wg, 0)
+    pre_gate[...] += product(x_full, wg, 1)
+    pre_up[...] = product(x_full, wu, 0)
+    pre_up[...] += product(x_full, wu, 1)
     loads[4].wait()
 
     pass_on(send_c, recv_c, zc_s, zc_r, tc_s, tc_r)
     own_c.wait()
+    assemble(recv_c, c_full, c)
+    d_own = product(c_full, wd, c)
     from_peer(send_c, recv_c, tc_s, tc_r)
-    assemble(recv_c, c_full)
-    d_hidden = jnp.dot(c_full[...], wd[...], preferred_element_type=F32)
+    assemble(recv_c, c_full, peer)
+    d_hidden = d_own + product(c_full, wd, peer)
     sigma = jax.nn.sigmoid(pre_gate[...])
     activated = pre_gate[...] * sigma
     width = hidden.shape[1]
@@ -190,91 +200,106 @@
 
     over_rows = (((0,), (0,)), ((), ()))
 
-    def weight_block(b, carry):
-        col = pl.multiple_of(b * 256, 256)
-        both = lax.dot_general(x_full[:, pl.ds(col, 256)], d_both[...], over_rows, preferred_element_type=F32)
-        down = lax.dot_general(c_full[:, pl.ds(col, 256)], hidden[...], over_rows, preferred_element_type=F32)
-        for m, value in enumerate((both[:, :width], both[:, width:], down)):
-            value = value.astype(BF16)
-            for k in range(NX):
-                for q in range(4):
-                    rows = value[k * 64 + q * 16 : k * 64 + q * 16 + 16, :]
-                    if q < 2:
-                        pa[b, q, k, m * 16 : m * 16 + 16, :] = rows
-                    else:
-                        pb[k, q - 2, b, m * 16 : m * 16 + 16, :] = rows
-        return carry
-
-    lax.fori_loop(0, NY, weight_block, 0)
+    def x_place(k):
+        gap = lax.rem(k - x + NX, NX)
+        return jnp.where(gap == 0, 3, jnp.where(gap == 1, 1, jnp.where(gap == 2, 0, 2)))
+
+    x_places = [x_place(k) for k in range(NX)]
+
+    def weight_block(j, carry):
+        offset = jnp.where(j % 2 == 0, -((NY - j) // 2), (NY - 1 - j) // 2)
+        b = lax.rem(y + offset + NY, NY)
+        side = b // (NY // 2)
+        col = pl.multiple_of(lax.rem(b, NY // 2) * 256, 256)
+        both = lax.dot_general(
+            x_full[side, :, pl.ds(col, 256)], d_both[...], over_rows, preferred_element_type=F32
+        )
+        down = lax.dot_general(
+            c_full[side, :, pl.ds(col, 256)], hidden[...], over_rows, preferred_element_type=F32
+        )
+        values = [v.astype(BF16) for v in (both[:, :width], both[:, width:], down)]
+        for k in range(NX):
+            for p in range(2):
+                for u, (q, m) in enumerate(A_UNITS[p]):
+                    row = k * 64 + q * 16
+                    parts_a[p][b, x_places[k], u * 16 : u * 16 + 16, :] = values[m][row : row + 16, :]
+                for u, (q, m) in enumerate(B_UNITS[p]):
+                    row = k * 64 + q * 16
+                    parts_b[p][k, j, u * 16 : u * 16 + 16, :] = values[m][row : row + 16, :]
+        return carry
 
     rings = {
-        "a": (NY, y, at_y, pa, ra, ra_s, ra_r),
-        "b": (NX, x, at_x, pb, rb, rb_s, rb_r),
-        "a2": (NX, x, at_x, pa2, ra2, ra2_s, ra2_r),
-        "b2": (NY, y, at_y, pb2, rb2, rb2_s, rb2_r),
+        "a": (NY, y, at_y, parts_a, slots_a, ra_s, ra_r, 2, 2),
+        "b": (NX, x, at_x, parts_b, slots_b, rb_s, rb_r, 4, 2),
+        "a2": (NX, x, at_x, parts_a2, slots_a2, ra2_s, ra2_r, 1, 1),
+        "b2": (NY, y, at_y, parts_b2, slots_b2, rb2_s, rb2_r, 1, 1),
     }
 
-    def hop(ring, chain, h):
-        n, me, at, parts, slots, send, recv = rings[ring]
-        sign, part, length, base = chain
+    def hop(ring, i, h, g):
+        n, me, at, parts, slots, send, recv, groups, size = rings[ring]
+        sign, part, length = chains_of(n)[i]
         target = lax.rem(me + n + sign, n)
         dest = lax.rem(me + n + sign * (length - h), n)
-        src = parts.at[dest, part] if h == 0 else slots.at[base + h - 1]
+        piece = pl.ds(g * size, size)
+        src = parts[part].at[dest, piece] if h == 0 else slots[i].at[h - 1, piece]
+        sem = (sum(l for _, _, l in chains_of(n)[:i]) + h) * groups + g
         return pltpu.make_async_remote_copy(
-            src_ref=src, dst_ref=slots.at[base + h], send_sem=send.at[base + h], recv_sem=recv.at[base + h],
+            src_ref=src, dst_ref=slots[i].at[h, piece], send_sem=send.at[sem], recv_sem=recv.at[sem],
             device_id=at(target), device_id_type=MESH,
         )
 
-    def begin(ring):
-        for chain in chains_of(rings[ring][0]):
-            hop(ring, chain, 0).start()
-
-    def serve(ring, which, h):
-        n, me, at, parts, slots, send, recv = rings[ring]
-        for chain in chains_of(n)[2 * which : 2 * which + 2]:
-            sign, part, length, base = chain
-            hop(ring, chain, h).wait_recv()
+    def begin(ring, which, g):
+        for i in which:
+            hop(ring, i, 0, g).start()
+
+    def serve(ring, which, h, g):
+        n, me, at, parts, slots, send, recv, groups, size = rings[ring]
+        for i in which:
+            sign, part, length = chains_of(n)[i]
+            hop(ring, i, h, g).wait_recv()
             if h < length - 1:
                 dest = lax.rem(me + n + sign * (length - h - 1), n)
-
-                def add(i, carry, base=base, h=h, dest=dest, part=part):
-                    total = slots[base + h, i].astype(F32) + parts[dest, part, i].astype(F32)
-                    slots[base + h, i] = total.astype(BF16)
-                    return carry
-
-                lax.fori_loop(0, parts.shape[2], add, 0)
-                hop(ring, chain, h + 1).start()
-
-    def finish(ring, store):
-        n, me, at, parts, slots, send, recv = rings[ring]
+                for k in range(g * size, g * size + size):
+                    total = slots[i][h, k].astype(F32) + parts[part][dest, k].astype(F32)
+                    slots[i][h, k] = total.astype(BF16)
+                hop(ring, i, h + 1, g).start()
+
+    def finish(ring, g, store):
+        n, me, at, parts, slots, send, recv, groups, size = rings[ring]
         for part in range(2):
-            last = [base + length - 1 for sign, p, length, base in chains_of(n) if p == part]
-
-            def one(i, carry, part=part, last=last):
-                store(
-                    part, i,
-                    parts[me, part, i].astype(F32) + slots[last[0], i].astype(F32) + slots[last[1], i].astype(F32),
-                )
-                return carry
-
-            lax.fori_loop(0, parts.shape[2], one, 0)
-
-    def to_a2(part, i, total):
-        pa2[i, part, 0] = total.astype(BF16)
-
-    def to_b2(part, i, total):
-        pb2[i, part, 0] = total.astype(BF16)
-
-    def to_out(first):
-        def store(part, i, total):
-            row = (first + part) * 16
-            for m, out in enumerate((out_gate, out_up, out_down)):
-                out[row : row + 16, :] = total[m * 16 : m * 16 + 16, :]
+            ends = [(i, l - 1) for i, (_, p, l) in enumerate(chains_of(n)) if p == part]
+            for k in range(g * size, g * size + size):
+                total = parts[part][me, k].astype(F32)
+                for i, h in ends:
+                    total = total + slots[i][h, k].astype(F32)
+                store(part, k, total)
+
+    def to_a2(part, k, total):
+        parts_a2[part][lax.rem(x + NX + X_ORDER[k], NX), 0] = total.astype(BF16)
+
+    def to_b2(part, k, total):
+        parts_b2[part][lax.rem(y + NY + Y_ORDER[k], NY), 0] = total.astype(BF16)
+
+    def to_out(units):
+        def store(part, k, total):
+            for u, (q, m) in enumerate(units[part]):
+                out = (out_gate, out_up, out_down)[m]
+                out[q * 16 : q * 16 + 16, :] = total[u * 16 : u * 16 + 16, :]
 
         return store
 
-    begin("a")
-    begin("b")
+    every, long, short = (0, 1, 2, 3), (0, 1), (2, 3)
+    lax.fori_loop(0, 2, weight_block, 0)
+    for g in range(2):
+        begin("a", long, g)
+    for g in range(2):
+        begin("a", (2,), g)
+    begin("b", every, 0)
+    lax.fori_loop(2, 4, weight_block, 0)
+    for g in range(2):
+        begin("a", (3,), g)
+    begin("b", every, 1)
+    lax.fori_loop(4, NY, weight_block, 0)
 
     over_width = (((1,), (1,)), ((), ()))
 
@@ -303,7 +328,8 @@
 
     lax.fori_loop(0, blocks, for_peer, 0)
     lax.fori_loop(0, blocks, for_own, 0)
-    serve("a", 0, 0)
+    serve("a", long, 0, 0)
+    serve("a", long, 0, 1)
 
     def join(b, carry):
         peer_copy(b).wait_recv()
@@ -329,31 +355,50 @@
     own_back = pltpu.make_async_copy(back_out.at[z], back_in.at[z], loc_sem.at[2])
     own_back.start()
 
-    serve("a", 1, 0)
-    serve("b", 0, 0)
-    serve("a", 0, 1)
-    serve("a", 1, 1)
-    serve("b", 1, 0)
-    serve("a", 0, 2)
-    serve("a", 1, 2)
-    serve("b", 0, 1)
-    finish("b", to_b2)
-    begin("b2")
-    serve("a", 0, 3)
-    finish("a", to_a2)
-    begin("a2")
-    serve("b2", 0, 0)
-    serve("b2", 1, 0)
-    serve("a2", 0, 0)
-    serve("a2", 1, 0)
-    serve("b2", 0, 1)
-    serve("b2", 1, 1)
-    serve("a2", 0, 1)
-    finish("a2", to_out(0))
-    serve("b2", 0, 2)
-    serve("b2", 1, 2)
-    serve("b2", 0, 3)
-    finish("b2", to_out(2))
+    serve("a", short, 0, 0)
+    serve("b", long, 0, 0)
+    begin("b", every, 2)
+    serve("a", short, 0, 1)
+    serve("a", long, 1, 0)
+    serve("b", short, 0, 0)
+    serve("b", long, 1, 0)
+    finish("b", 0, to_b2)
+    begin("b2", (0, 1, 2), 0)
+    serve("a", long, 1, 1)
+    serve("b", long, 0, 1)
+    begin("b", every, 3)
+    serve("a", short, 1, 0)
+    serve("a", short, 1, 1)
+    serve("a", long, 2, 0)
+    serve("b", short, 0, 1)
+    serve("b", long, 1, 1)
+    finish("b", 1, to_b2)
+    begin("b2", (3,), 0)
+    serve("b2", (0, 1, 2), 0, 0)
+    serve("a", long, 2, 1)
+    serve("b", long, 0, 2)
+    serve("a", short, 2, 0)
+    serve("a", short, 2, 1)
+    serve("b2", (0,), 1, 0)
+    serve("b", short, 0, 2)
+    serve("b", long, 1, 2)
+    finish("b", 2, to_b2)
+    serve("b2", (3,), 0, 0)
+    serve("b2", (1, 2), 1, 0)
+    serve("b2", (0,), 2, 0)
+    serve("b", long, 0, 3)
+    serve("a", long, 3, 0)
+    finish("a", 0, to_a2)
+    begin("a2", (0, 1, 2), 0)
+    serve("a", long, 3, 1)
+    finish("a", 1, to_a2)
+    begin("a2", (3,), 0)
+    serve("b", short, 0, 3)
+    serve("b", long, 1, 3)
+    finish("b", 3, to_b2)
+    serve("b2", (1,), 2, 0)
+    serve("b2", (3,), 1, 0)
+    serve("a2", long, 0, 0)
 
     def arrived(i, carry):
         back_copy(turn(i), turn(i)).wait_recv()
@@ -366,12 +411,22 @@
         col = pl.multiple_of(b * 256, 256)
         rows = [back_in[e, :, pl.ds(col, 256)].astype(F32) for e in range(NZ)]
         rows = jnp.concatenate(rows, axis=0).astype(BF16)
-        out_tok[:, pl.ds(col, 256)] = lax.dot_general(
+        tok_grad[:, pl.ds(col, 256)] = lax.dot_general(
             place[...], rows, over_rows, preferred_element_type=F32
         ).astype(BF16)
         return carry
 
     lax.fori_loop(0, blocks, token_block, 0)
+    tok_out = pltpu.make_async_copy(tok_grad, out_tok, loc_sem.at[3])
+    tok_out.start()
+
+    serve("a2", short, 0, 0)
+    serve("a2", long, 1, 0)
+    finish("a2", 0, to_out(A_UNITS))
+    serve("b2", (0, 1), 3, 0)
+    serve("b2", (2, 3), 2, 0)
+    finish("b2", 0, to_out(B_UNITS))
+    tok_out.wait()
 
     def sent(i, carry):
         target = turn(i)
@@ -395,9 +450,24 @@
 
     lax.fori_loop(0, blocks, sent_blocks, 0)
     for ring in rings:
-        for chain in chains_of(rings[ring][0]):
+        n, groups = rings[ring][0], rings[ring][7]
+        for i, chain in enumerate(chains_of(n)):
             for h in range(chain[2]):
-                hop(ring, chain, h).wait_send()
+                for g in range(groups):
+                    hop(ring, i, h, g).wait_send()
+
+
+def finish_kernel(a, b, c, d, out_a, out_b, out_c, out_d, held_a, held_b, held_c, held_d, in_sems, out_sems):
+    sources, outs, held = (a, b, c, d), (out_a, out_b, out_c, out_d), (held_a, held_b, held_c, held_d)
+    loads = [pltpu.make_async_copy(src, buf, in_sems.at[i]) for i, (src, buf) in enumerate(zip(sources, held))]
+    stores = [pltpu.make_async_copy(buf, out, out_sems.at[i]) for i, (buf, out) in enumerate(zip(held, outs))]
+    for load in loads:
+        load.start()
+    for load, store in zip(loads, stores):
+        load.wait()
+        store.start()
+    for store in stores:
+        store.wait()
 
 
 def per_device(tokens, cotangent, route_ids, gate_codes, w_gate, w_up, w_down):
@@ -406,41 +476,56 @@
     dma = lambda n: pltpu.SemaphoreType.DMA((n,))
     vm = pltpu.VMEM
     a_hops, b_hops = NY - 1, NX - 1
+
+    def parts_of(n, blocks, units):
+        return [vm((n, blocks, 16 * len(u), width), BF16) for u in units]
+
+    def slots_of(n, blocks, units):
+        return [vm((length, blocks, 16 * len(units[part]), width), BF16) for _, part, length in chains_of(n)]
+
     scratch = [
         vm((rows, cols), BF16), vm((rows, cols), BF16),
         vm((depth, width), BF16), vm((depth, width), BF16), vm((depth, width), BF16),
         vm((SLOTS, rows), BF16),
         vm((NZ, CAP, cols), BF16), vm((NZ, CAP, cols), BF16),
         vm((2, NZ, CAP, cols), BF16), vm((2, NZ, CAP, cols), BF16),
-        vm((SLOTS, depth), BF16), vm((SLOTS, depth), BF16),
+        vm((2, SLOTS, cols), BF16), vm((2, SLOTS, cols), BF16),
         vm((SLOTS, width), F32), vm((SLOTS, width), F32),
         vm((SLOTS, 2 * width), BF16), vm((SLOTS, width), BF16),
         vm((cols // 256, SLOTS, 256), F32), vm((cols // 256, SLOTS, 256), BF16), vm((cols // 256, SLOTS, 256), BF16),
         vm((NZ, CAP, cols), BF16), vm((NZ, CAP, cols), BF16),
-        vm((NY, 2, NX, 48, width), BF16), vm((NX, 2, NY, 48, width), BF16),
-        vm((NX, 2, 1, 48, width), BF16), vm((NY, 2, 1, 48, width), BF16),
-        vm((2 * a_hops, NX, 48, width), BF16), vm((2 * b_hops, NY, 48, width), BF16),
-        vm((2 * b_hops, 1, 48, width), BF16), vm((2 * a_hops, 1, 48, width), BF16),
-        dma(5), dma(NZ), dma(NZ), dma(NZ), dma(NZ), dma(NZ), dma(NZ), dma(NZ), dma(NZ), dma(3),
+        vm((rows, cols), BF16),
+        parts_of(NY, NX, A_UNITS), parts_of(NX, NY, B_UNITS), parts_of(NX, 1, A_UNITS), parts_of(NY, 1, B_UNITS),
+        slots_of(NY, NX, A_UNITS), slots_of(NX, NY, B_UNITS), slots_of(NX, 1, A_UNITS), slots_of(NY, 1, B_UNITS),
+        dma(5), dma(NZ), dma(NZ), dma(NZ), dma(NZ), dma(NZ), dma(NZ), dma(NZ), dma(NZ), dma(4),
         dma(4), dma(4), dma(NZ), dma(NZ),
-        dma(2 * a_hops), dma(2 * a_hops), dma(2 * b_hops), dma(2 * b_hops),
+        dma(4 * a_hops), dma(4 * a_hops), dma(8 * b_hops), dma(8 * b_hops),
         dma(2 * b_hops), dma(2 * b_hops), dma(2 * a_hops), dma(2 * a_hops),
     ]
     in_vmem = pl.BlockSpec(memory_space=pltpu.VMEM)
     anywhere = pl.BlockSpec(memory_space=pl.ANY)
     out_rows = depth // (NX * NY)
     weight_out = jax.ShapeDtypeStruct((out_rows, width), F32)
-    token_grad, grad_gate, grad_up, grad_down = pl.pallas_call(
+    results = (jax.ShapeDtypeStruct((rows, cols), BF16), weight_out, weight_out, weight_out)
+    made = pl.pallas_call(
         kernel,
-        out_shape=(jax.ShapeDtypeStruct((rows, cols), BF16), weight_out, weight_out, weight_out),
+        out_shape=results,
         in_specs=[in_vmem, in_vmem] + [anywhere] * 5,
-        out_specs=(in_vmem,) * 4,
+        out_specs=(anywhere, in_vmem, in_vmem, in_vmem),
         scratch_shapes=scratch,
         compiler_params=pltpu.CompilerParams(
             collective_id=0, has_side_effects=True, vmem_limit_bytes=56 * 1024 * 1024
         ),
         name="moe_backward",
     )(route_ids.T, gate_codes.T, tokens, cotangent, w_gate[0], w_up[0], w_down[0])
+    token_grad, grad_gate, grad_up, grad_down = pl.pallas_call(
+        finish_kernel,
+        out_shape=results,
+        in_specs=[anywhere] * 4,
+        out_specs=(anywhere,) * 4,
+        scratch_shapes=[vm(r.shape, r.dtype) for r in results] + [dma(4), dma(4)],
+        name="moe_outputs",
+    )(*made)
     return token_grad, grad_gate[None], grad_up[None], grad_down[None]
 
 

time: 113 us -> 104 us (0.920); the launches traced: 111 us -> 103 us
  local copies, waits for them, and re-layouts: 6.48 us -> 0 us
    unnamed x4 -> x0, local copies, waits for them, and re-layouts: 6.48 us -> none
    pallas_call x1 -> x2, Pallas kernels: 104 us -> 103 us  [the longest x1 101 us: per_device(): pl.pallas_call(kernel, out_shape=results, in_specs=[in_vmem, in_vmem] + [...]
where the time goes in v2:
time: 104 us; the launch traced here: 103 us
  Pallas kernels  103 us (99%)
    pallas_call x1, Pallas kernels, per_device(): pl.pallas_call(kernel, out_shape=results, in_specs=[in_vmem, in_vmem] + [...  101 us

profile of v2, /device:TPU:1, one launch (start us, length us, event | category | flops | bytes accessed | tf_op | source)
XLA Modules:
  0.0 103.5 jit_solution(10782491134921723639)
XLA Ops:
  0.6 100.9 %moe_backward.1 = (bf16[256,1024]{1,0:T(8,128)(2,1)}, f32[64,384]{1,0:T(8,128)}, f32[64,384]{1,0:T(8,128)}, f32[64,384]{1,0:T(8,128)}) custom-call(s32[8,256]{1,0:T(8,128)} %bitcast.11, s32[8,256]{1,0:T(8,128)} %bitcast.12, bf16[256,1024]{1,0:T(8,128)(2,1)} %tok_hbm.1, bf16[256,1024]{1,0:T(8,128)(2,1)} %cot_hbm.1, bf16[2048,384]{1,0:T(8,128)(2,1)} %bitcast.8, ...), custom_call_target="tpu_custom_call" | custom-call | tf_op jit(solution)/shard_map/moe_backward/pallas_call | solution.py:510
  101.5 2.0 %moe_outputs.1 = (bf16[256,1024]{1,0:T(8,128)(2,1)}, f32[64,384]{1,0:T(8,128)}, f32[64,384]{1,0:T(8,128)}, f32[64,384]{1,0:T(8,128)}) custom-call(bf16[256,1024]{1,0:T(8,128)(2,1)} %get-tuple-element.12.a, f32[64,384]{1,0:T(8,128)} %get-tuple-element.13.b, f32[64,384]{1,0:T(8,128)} %get-tuple-element.14.c, f32[64,384]{1,0:T(8,128)} %get-tuple-element.15.d), custom_call_target="tpu_custom_call" | custom-call | tf_op jit(solution)/shard_map/moe_outputs/pallas_call | solution.py:521

commit v3 on v2

--- a/solution.py
+++ b/solution.py
@@ -30,7 +30,7 @@
 def kernel(
     ids_ref, codes_ref, tok_hbm, cot_hbm, wg_hbm, wu_hbm, wd_hbm,
     out_tok, out_gate, out_up, out_down,
-    tok, cot, wg, wu, wd, place, send_x, send_c, recv_x, recv_c, x_full, c_full, pre_gate, pre_up,
+    tok, cot, wg, wu, wd, place, send_x, send_c, recv_x, recv_c, x_full, c_full, to_gate, to_up,
     d_both, hidden, own_part, peer_out, peer_in, back_out, back_in, tok_grad,
     parts_a, parts_b, parts_a2, parts_b2, slots_a, slots_b, slots_a2, slots_b2,
     in_sem, zx_s, zx_r, zc_s, zc_r, tx_s, tx_r, tc_s, tc_r, loc_sem, p_s, p_r, back_s, back_r,
@@ -77,11 +77,9 @@
     count = ids_ref.shape[1]
     expert_row = lax.broadcasted_iota(jnp.int32, (16, count), 0)
     match = jnp.zeros((16, count), F32)
-    gates = jnp.zeros((16, count), F32)
     for k in range(ids_ref.shape[0]):
         same = ids_ref[k : k + 1, :] == expert_row
         match = match + jnp.where(same, 1.0, 0.0)
-        gates = gates + jnp.where(same, codes_ref[k : k + 1, :].astype(F32) / GATE_UNIT, 0.0)
     before = jnp.where(
         lax.broadcasted_iota(jnp.int32, (count, count), 0) < lax.broadcasted_iota(jnp.int32, (count, count), 1),
         1.0, 0.0,
@@ -89,13 +87,8 @@
     position = jnp.dot(match.astype(BF16), before, preferred_element_type=F32)
     position = jnp.where(match > 0.5, position, -1.0)
     slot_row = lax.broadcasted_iota(jnp.int32, (CAP, count), 0).astype(F32)
-    pieces, slot_gates = [], []
-    for e in range(NZ):
-        piece = jnp.where(position[e : e + 1, :] == slot_row, 1.0, 0.0)
-        pieces.append(piece)
-        slot_gates.append(jnp.sum(piece * gates[e : e + 1, :], axis=1, keepdims=True))
+    pieces = [jnp.where(position[e : e + 1, :] == slot_row, 1.0, 0.0) for e in range(NZ)]
     place[...] = jnp.concatenate(pieces, axis=0).astype(BF16)
-    slot_gate = jnp.concatenate(slot_gates, axis=0)
 
     def z_copy(src, dst, send, recv, target, slab):
         return pltpu.make_async_remote_copy(
@@ -136,6 +129,17 @@
     gather(tok, send_x, None)
     pl.semaphore_wait(barrier, NZ - 1 + 5)
     own_x = send_all(send_x, recv_x, zx_s, zx_r, tx_s, tx_r, 0)
+    gates = jnp.zeros((16, count), F32)
+    for k in range(ids_ref.shape[0]):
+        same = ids_ref[k : k + 1, :] == expert_row
+        gates = gates + jnp.where(same, codes_ref[k : k + 1, :].astype(F32) / GATE_UNIT, 0.0)
+    slot_gate = jnp.concatenate(
+        [
+            jnp.sum(place[e * CAP : (e + 1) * CAP, :].astype(F32) * gates[e : e + 1, :], axis=1, keepdims=True)
+            for e in range(NZ)
+        ],
+        axis=0,
+    )
     loads[1].wait()
     gather(cot, send_c, slot_gate)
     own_c = send_all(send_c, recv_c, zc_s, zc_r, tc_s, tc_r, 1)
@@ -176,10 +180,14 @@
     loads[3].wait()
     assemble(recv_x, x_full, 0)
     assemble(recv_x, x_full, 1)
-    pre_gate[...] = product(x_full, wg, 0)
-    pre_gate[...] += product(x_full, wg, 1)
-    pre_up[...] = product(x_full, wu, 0)
-    pre_up[...] += product(x_full, wu, 1)
+    gate = product(x_full, wg, 0) + product(x_full, wg, 1)
+    up = product(x_full, wu, 0) + product(x_full, wu, 1)
+    width = hidden.shape[1]
+    sigma = jax.nn.sigmoid(gate)
+    activated = gate * sigma
+    hidden[...] = (activated * up).astype(BF16)
+    to_gate[...] = up * sigma * (1.0 + gate * (1.0 - sigma))
+    to_up[...] = activated
     loads[4].wait()
 
     pass_on(send_c, recv_c, zc_s, zc_r, tc_s, tc_r)
@@ -189,14 +197,8 @@
     from_peer(send_c, recv_c, tc_s, tc_r)
     assemble(recv_c, c_full, peer)
     d_hidden = d_own + product(c_full, wd, peer)
-    sigma = jax.nn.sigmoid(pre_gate[...])
-    activated = pre_gate[...] * sigma
-    width = hidden.shape[1]
-    hidden[...] = (activated * pre_up[...]).astype(BF16)
-    d_both[:, :width] = (
-        d_hidden * pre_up[...] * sigma * (1.0 + pre_gate[...] * (1.0 - sigma))
-    ).astype(BF16)
-    d_both[:, width:] = (d_hidden * activated).astype(BF16)
+    d_both[:, :width] = (d_hidden * to_gate[...]).astype(BF16)
+    d_both[:, width:] = (d_hidden * to_up[...]).astype(BF16)
 
     over_rows = (((0,), (0,)), ((), ()))
 
@@ -289,17 +291,6 @@
         return store
 
     every, long, short = (0, 1, 2, 3), (0, 1), (2, 3)
-    lax.fori_loop(0, 2, weight_block, 0)
-    for g in range(2):
-        begin("a", long, g)
-    for g in range(2):
-        begin("a", (2,), g)
-    begin("b", every, 0)
-    lax.fori_loop(2, 4, weight_block, 0)
-    for g in range(2):
-        begin("a", (3,), g)
-    begin("b", every, 1)
-    lax.fori_loop(4, NY, weight_block, 0)
 
     over_width = (((1,), (1,)), ((), ()))
 
@@ -326,7 +317,14 @@
         own_part[b] = route_block(c * cols + b * 256)
         return carry
 
+    lax.fori_loop(0, 3, weight_block, 0)
+    for which in (long, short):
+        for g in range(2):
+            begin("a", which, g)
+    begin("b", every, 0)
     lax.fori_loop(0, blocks, for_peer, 0)
+    lax.fori_loop(3, 5, weight_block, 0)
+    begin("b", every, 1)
     lax.fori_loop(0, blocks, for_own, 0)
     serve("a", long, 0, 0)
     serve("a", long, 0, 1)
@@ -354,6 +352,7 @@
     lax.fori_loop(1, NZ, send_back, 0)
     own_back = pltpu.make_async_copy(back_out.at[z], back_in.at[z], loc_sem.at[2])
     own_back.start()
+    lax.fori_loop(5, NY, weight_block, 0)
 
     serve("a", short, 0, 0)
     serve("b", long, 0, 0)

time: 104 us -> 104 us (level)
  the two profiles are of different devices: /device:TPU:1 before, /device:TPU:64 now
where the time goes in v3:
time: 104 us
  Pallas kernels  103 us (99%)
    pallas_call x1, Pallas kernels, per_device(): pl.pallas_call(kernel, out_shape=results, in_specs=[in_vmem, in_vmem] + [...  101 us

profile of v3, /device:TPU:64, one launch (start us, length us, event | category | flops | bytes accessed | tf_op | source)
XLA Modules:
  0.0 103.7 jit_solution(1038045734957261527)
XLA Ops:
  0.6 101.1 %moe_backward.1 = (bf16[256,1024]{1,0:T(8,128)(2,1)}, f32[64,384]{1,0:T(8,128)}, f32[64,384]{1,0:T(8,128)}, f32[64,384]{1,0:T(8,128)}) custom-call(s32[8,256]{1,0:T(8,128)} %bitcast.11, s32[8,256]{1,0:T(8,128)} %bitcast.12, bf16[256,1024]{1,0:T(8,128)(2,1)} %tok_hbm.1, bf16[256,1024]{1,0:T(8,128)(2,1)} %cot_hbm.1, bf16[2048,384]{1,0:T(8,128)(2,1)} %bitcast.8, ...), custom_call_target="tpu_custom_call" | custom-call | tf_op jit(solution)/shard_map/moe_backward/pallas_call | solution.py:509
  101.8 2.0 %moe_outputs.1 = (bf16[256,1024]{1,0:T(8,128)(2,1)}, f32[64,384]{1,0:T(8,128)}, f32[64,384]{1,0:T(8,128)}, f32[64,384]{1,0:T(8,128)}) custom-call(bf16[256,1024]{1,0:T(8,128)(2,1)} %get-tuple-element.12.a, f32[64,384]{1,0:T(8,128)} %get-tuple-element.13.b, f32[64,384]{1,0:T(8,128)} %get-tuple-element.14.c, f32[64,384]{1,0:T(8,128)} %get-tuple-element.15.d), custom_call_target="tpu_custom_call" | custom-call | tf_op jit(solution)/shard_map/moe_outputs/pallas_call | solution.py:520

commit v4 on v3

--- a/solution.py
+++ b/solution.py
@@ -14,6 +14,7 @@
 CAP = 24
 SLOTS = NZ * CAP
 GATE_UNIT = 65536.0
+VLIM = 56
 
 
 Y_ORDER = (4, 3, -3, 2, -2, 1, -1, 0)
@@ -43,11 +44,20 @@
     peer = 1 - c
     cols = tok.shape[1]
 
-    loads = [
-        pltpu.make_async_copy(src, dst, in_sem.at[i])
-        for i, (src, dst) in enumerate(((tok_hbm, tok), (cot_hbm, cot), (wg_hbm, wg), (wu_hbm, wu), (wd_hbm, wd)))
+    def in_blocks(src, dst, first):
+        size = dst.shape[0] // 4
+        return [
+            pltpu.make_async_copy(
+                src.at[i * size : (i + 1) * size], dst.at[i * size : (i + 1) * size], in_sem.at[first + i]
+            )
+            for i in range(4)
+        ]
+
+    tok_loads, cot_loads = in_blocks(tok_hbm, tok, 0), in_blocks(cot_hbm, cot, 4)
+    weight_loads = [
+        pltpu.make_async_copy(src, dst, in_sem.at[8 + i]) for i, (src, dst) in enumerate(((wg_hbm, wg), (wu_hbm, wu), (wd_hbm, wd)))
     ]
-    for load in loads:
+    for load in tok_loads:
         load.start()
 
     def at_z(k):
@@ -103,7 +113,7 @@
         )
 
     def turn(i):
-        step = (i + 1) // 2
+        step = (NZ + 1 - i) // 2
         return lax.rem(z + NZ + jnp.where(i % 2 == 1, step, -step), NZ)
 
     def gather(table, buffer, scale):
@@ -125,7 +135,10 @@
         own_copy.start()
         return own_copy
 
-    loads[0].wait()
+    for load in tok_loads:
+        load.wait()
+    for load in cot_loads:
+        load.start()
     gather(tok, send_x, None)
     pl.semaphore_wait(barrier, NZ - 1 + 5)
     own_x = send_all(send_x, recv_x, zx_s, zx_r, tx_s, tx_r, 0)
@@ -140,65 +153,73 @@
         ],
         axis=0,
     )
-    loads[1].wait()
+    for load in cot_loads:
+        load.wait()
+    for load in weight_loads:
+        load.start()
     gather(cot, send_c, slot_gate)
     own_c = send_all(send_c, recv_c, zc_s, zc_r, tc_s, tc_r, 1)
 
-    def pass_on(src, dst, zs, zr, ts, tr):
+    slab_of = [z] + [turn(i) for i in range(1, NZ)]
+
+    def pass_on(src, dst, zs, zr, ts, tr, low, high):
         def one(i, carry):
             slab = turn(i)
             z_copy(src, dst, zs, zr, slab, slab).wait_recv()
             t_copy(dst.at[c, slab], dst, c, ts, tr, slab).start()
             return carry
 
-        lax.fori_loop(1, NZ, one, 0)
-
-    def from_peer(src, dst, ts, tr):
+        lax.fori_loop(low, high, one, 0)
+
+    def from_peer(src, dst, ts, tr, low, high):
         def one(i, carry):
-            t_copy(src.at[i], dst, peer, ts, tr, i).wait_recv()
+            slab = jnp.where(i == 0, z, turn(i))
+            t_copy(src.at[slab], dst, peer, ts, tr, slab).wait_recv()
             return carry
 
-        lax.fori_loop(0, NZ, one, 0)
-
-    def assemble(slabs, full, half):
+        lax.fori_loop(low, high, one, 0)
+
+    def assemble(slabs, full, half, low, high):
         def one(b, carry):
             col = pl.multiple_of(b * 256, 256)
-            rows = [slabs[half, e, :, pl.ds(col, 256)].astype(F32) for e in range(NZ)]
-            full[half, :, pl.ds(col, 256)] = jnp.concatenate(rows, axis=0).astype(BF16)
+            rows = [slabs[half, slab_of[i], :, pl.ds(col, 256)].astype(F32) for i in range(low, high)]
+            full[half, low * CAP : high * CAP, pl.ds(col, 256)] = jnp.concatenate(rows, axis=0).astype(BF16)
             return carry
 
         lax.fori_loop(0, cols // 256, one, 0)
 
-    def product(full, weights, half):
+    def product(full, weights, half, low, high):
         rows = pl.ds(pl.multiple_of(half * cols, cols), cols)
-        return jnp.dot(full[half], weights[rows, :], preferred_element_type=F32)
-
-    pass_on(send_x, recv_x, zx_s, zx_r, tx_s, tx_r)
+        return jnp.dot(full[half, low * CAP : high * CAP, :], weights[rows, :], preferred_element_type=F32)
+
+    pass_on(send_x, recv_x, zx_s, zx_r, tx_s, tx_r, 1, NZ)
     own_x.wait()
-    from_peer(send_x, recv_x, tx_s, tx_r)
-    loads[2].wait()
-    loads[3].wait()
-    assemble(recv_x, x_full, 0)
-    assemble(recv_x, x_full, 1)
-    gate = product(x_full, wg, 0) + product(x_full, wg, 1)
-    up = product(x_full, wu, 0) + product(x_full, wu, 1)
+    from_peer(send_x, recv_x, tx_s, tx_r, 0, NZ)
+    weight_loads[0].wait()
+    weight_loads[1].wait()
+    assemble(recv_x, x_full, 0, 0, NZ)
+    assemble(recv_x, x_full, 1, 0, NZ)
+    gate = product(x_full, wg, 0, 0, NZ) + product(x_full, wg, 1, 0, NZ)
+    up = product(x_full, wu, 0, 0, NZ) + product(x_full, wu, 1, 0, NZ)
     width = hidden.shape[1]
     sigma = jax.nn.sigmoid(gate)
     activated = gate * sigma
     hidden[...] = (activated * up).astype(BF16)
     to_gate[...] = up * sigma * (1.0 + gate * (1.0 - sigma))
     to_up[...] = activated
-    loads[4].wait()
-
-    pass_on(send_c, recv_c, zc_s, zc_r, tc_s, tc_r)
+    weight_loads[2].wait()
+
     own_c.wait()
-    assemble(recv_c, c_full, c)
-    d_own = product(c_full, wd, c)
-    from_peer(send_c, recv_c, tc_s, tc_r)
-    assemble(recv_c, c_full, peer)
-    d_hidden = d_own + product(c_full, wd, peer)
-    d_both[:, :width] = (d_hidden * to_gate[...]).astype(BF16)
-    d_both[:, width:] = (d_hidden * to_up[...]).astype(BF16)
+    for low, high in ((0, NZ // 2), (NZ // 2, NZ)):
+        pass_on(send_c, recv_c, zc_s, zc_r, tc_s, tc_r, max(low, 1), high)
+        assemble(recv_c, c_full, c, low, high)
+        d_own = product(c_full, wd, c, low, high)
+        from_peer(send_c, recv_c, tc_s, tc_r, low, high)
+        assemble(recv_c, c_full, peer, low, high)
+        d_hidden = d_own + product(c_full, wd, peer, low, high)
+        held = slice(low * CAP, high * CAP)
+        d_both[held, :width] = (d_hidden * to_gate[held, :]).astype(BF16)
+        d_both[held, width:] = (d_hidden * to_up[held, :]).astype(BF16)
 
     over_rows = (((0,), (0,)), ((), ()))
 
@@ -317,10 +338,12 @@
         own_part[b] = route_block(c * cols + b * 256)
         return carry
 
-    lax.fori_loop(0, 3, weight_block, 0)
-    for which in (long, short):
-        for g in range(2):
-            begin("a", which, g)
+    lax.fori_loop(0, 1, weight_block, 0)
+    for g in range(2):
+        begin("a", long, g)
+    lax.fori_loop(1, 3, weight_block, 0)
+    for g in range(2):
+        begin("a", short, g)
     begin("b", every, 0)
     lax.fori_loop(0, blocks, for_peer, 0)
     lax.fori_loop(3, 5, weight_block, 0)
@@ -334,7 +357,7 @@
         total = (own_part[b] + peer_in[b].astype(F32))
         col = pl.multiple_of(b * 256, 256)
         for e in range(NZ):
-            back_out[e, :, pl.ds(col, 256)] = total[e * CAP : (e + 1) * CAP, :].astype(BF16)
+            back_out[slab_of[e], :, pl.ds(col, 256)] = total[e * CAP : (e + 1) * CAP, :].astype(BF16)
         return carry
 
     lax.fori_loop(0, blocks, join, 0)
@@ -457,9 +480,13 @@
 
 
 def finish_kernel(a, b, c, d, out_a, out_b, out_c, out_d, held_a, held_b, held_c, held_d, in_sems, out_sems):
-    sources, outs, held = (a, b, c, d), (out_a, out_b, out_c, out_d), (held_a, held_b, held_c, held_d)
-    loads = [pltpu.make_async_copy(src, buf, in_sems.at[i]) for i, (src, buf) in enumerate(zip(sources, held))]
-    stores = [pltpu.make_async_copy(buf, out, out_sems.at[i]) for i, (buf, out) in enumerate(zip(held, outs))]
+    moves = [(b, held_b, out_b), (c, held_c, out_c), (d, held_d, out_d)]
+    size = a.shape[0] // 4
+    for i in range(4):
+        part = pl.ds(i * size, size)
+        moves.append((a.at[part], held_a.at[part], out_a.at[part]))
+    loads = [pltpu.make_async_copy(src, buf, in_sems.at[i]) for i, (src, buf, _) in enumerate(moves)]
+    stores = [pltpu.make_async_copy(buf, out, out_sems.at[i]) for i, (_, buf, out) in enumerate(moves)]
     for load in loads:
         load.start()
     for load, store in zip(loads, stores):
@@ -496,7 +523,7 @@
         vm((rows, cols), BF16),
         parts_of(NY, NX, A_UNITS), parts_of(NX, NY, B_UNITS), parts_of(NX, 1, A_UNITS), parts_of(NY, 1, B_UNITS),
         slots_of(NY, NX, A_UNITS), slots_of(NX, NY, B_UNITS), slots_of(NX, 1, A_UNITS), slots_of(NY, 1, B_UNITS),
-        dma(5), dma(NZ), dma(NZ), dma(NZ), dma(NZ), dma(NZ), dma(NZ), dma(NZ), dma(NZ), dma(4),
+        dma(11), dma(NZ), dma(NZ), dma(NZ), dma(NZ), dma(NZ), dma(NZ), dma(NZ), dma(NZ), dma(4),
         dma(4), dma(4), dma(NZ), dma(NZ),
         dma(4 * a_hops), dma(4 * a_hops), dma(8 * b_hops), dma(8 * b_hops),
         dma(2 * b_hops), dma(2 * b_hops), dma(2 * a_hops), dma(2 * a_hops),
@@ -513,7 +540,7 @@
         out_specs=(anywhere, in_vmem, in_vmem, in_vmem),
         scratch_shapes=scratch,
         compiler_params=pltpu.CompilerParams(
-            collective_id=0, has_side_effects=True, vmem_limit_bytes=56 * 1024 * 1024
+            collective_id=0, has_side_effects=True, vmem_limit_bytes=VLIM * 1024 * 1024
         ),
         name="moe_backward",
     )(route_ids.T, gate_codes.T, tokens, cotangent, w_gate[0], w_up[0], w_down[0])
@@ -522,7 +549,7 @@
         out_shape=results,
         in_specs=[anywhere] * 4,
         out_specs=(anywhere,) * 4,
-        scratch_shapes=[vm(r.shape, r.dtype) for r in results] + [dma(4), dma(4)],
+        scratch_shapes=[vm(r.shape, r.dtype) for r in results] + [dma(7), dma(7)],
         name="moe_outputs",
     )(*made)
     return token_grad, grad_gate[None], grad_up[None], grad_down[None]

time: 104 us -> 101 us (0.971)
  the two profiles are of different devices: /device:TPU:64 before, /device:TPU:1 now
where the time goes in v4:
time: 101 us; the launch traced here: 99.8 us
  Pallas kernels  99.1 us (98%)
    pallas_call x1, Pallas kernels, per_device(): pl.pallas_call(kernel, out_shape=results, in_specs=[in_vmem, in_vmem] + [...  97.1 us

profile of v4, /device:TPU:1, one launch (start us, length us, event | category | flops | bytes accessed | tf_op | source)
XLA Modules:
  0.0 99.8 jit_solution(15411009762189095452)
XLA Ops:
  0.6 97.1 %moe_backward.1 = (bf16[256,1024]{1,0:T(8,128)(2,1)}, f32[64,384]{1,0:T(8,128)}, f32[64,384]{1,0:T(8,128)}, f32[64,384]{1,0:T(8,128)}) custom-call(s32[8,256]{1,0:T(8,128)} %bitcast.11, s32[8,256]{1,0:T(8,128)} %bitcast.12, bf16[256,1024]{1,0:T(8,128)(2,1)} %tok_hbm.1, bf16[256,1024]{1,0:T(8,128)(2,1)} %cot_hbm.1, bf16[2048,384]{1,0:T(8,128)(2,1)} %bitcast.8, ...), custom_call_target="tpu_custom_call" | custom-call | tf_op jit(solution)/shard_map/moe_backward/pallas_call | solution.py:536
  97.8 2.0 %moe_outputs.1 = (bf16[256,1024]{1,0:T(8,128)(2,1)}, f32[64,384]{1,0:T(8,128)}, f32[64,384]{1,0:T(8,128)}, f32[64,384]{1,0:T(8,128)}) custom-call(bf16[256,1024]{1,0:T(8,128)(2,1)} %get-tuple-element.12.a, f32[64,384]{1,0:T(8,128)} %get-tuple-element.13.b, f32[64,384]{1,0:T(8,128)} %get-tuple-element.14.c, f32[64,384]{1,0:T(8,128)} %get-tuple-element.15.d), custom_call_target="tpu_custom_call" | custom-call | tf_op jit(solution)/shard_map/moe_outputs/pallas_call | solution.py:547

commit v5 on v4

--- a/solution.py
+++ b/solution.py
@@ -341,10 +341,13 @@
     lax.fori_loop(0, 1, weight_block, 0)
     for g in range(2):
         begin("a", long, g)
-    lax.fori_loop(1, 3, weight_block, 0)
+    lax.fori_loop(1, 2, weight_block, 0)
+    begin("b", every, 0)
     for g in range(2):
-        begin("a", short, g)
-    begin("b", every, 0)
+        begin("a", (2,), g)
+    lax.fori_loop(2, 3, weight_block, 0)
+    for g in range(2):
+        begin("a", (3,), g)
     lax.fori_loop(0, blocks, for_peer, 0)
     lax.fori_loop(3, 5, weight_block, 0)
     begin("b", every, 1)

time: 101 us -> 101 us (level)
  the two profiles are of different devices: /device:TPU:1 before, /device:TPU:2 now
where the time goes in v5:
time: 101 us
  Pallas kernels  100 us (99%)
    pallas_call x1, Pallas kernels, per_device(): pl.pallas_call(kernel, out_shape=results, in_specs=[in_vmem, in_vmem] + [...  98.2 us

profile of v5, /device:TPU:2, one launch (start us, length us, event | category | flops | bytes accessed | tf_op | source)
XLA Modules:
  0.0 100.8 jit_solution(6476513381877857545)
XLA Ops:
  0.6 98.2 %moe_backward.1 = (bf16[256,1024]{1,0:T(8,128)(2,1)}, f32[64,384]{1,0:T(8,128)}, f32[64,384]{1,0:T(8,128)}, f32[64,384]{1,0:T(8,128)}) custom-call(s32[8,256]{1,0:T(8,128)} %bitcast.11, s32[8,256]{1,0:T(8,128)} %bitcast.12, bf16[256,1024]{1,0:T(8,128)(2,1)} %tok_hbm.1, bf16[256,1024]{1,0:T(8,128)(2,1)} %cot_hbm.1, bf16[2048,384]{1,0:T(8,128)(2,1)} %bitcast.8, ...), custom_call_target="tpu_custom_call" | custom-call | tf_op jit(solution)/shard_map/moe_backward/pallas_call | solution.py:539
  98.8 2.0 %moe_outputs.1 = (bf16[256,1024]{1,0:T(8,128)(2,1)}, f32[64,384]{1,0:T(8,128)}, f32[64,384]{1,0:T(8,128)}, f32[64,384]{1,0:T(8,128)}) custom-call(bf16[256,1024]{1,0:T(8,128)(2,1)} %get-tuple-element.12.a, f32[64,384]{1,0:T(8,128)} %get-tuple-element.13.b, f32[64,384]{1,0:T(8,128)} %get-tuple-element.14.c, f32[64,384]{1,0:T(8,128)} %get-tuple-element.15.d), custom_call_target="tpu_custom_call" | custom-call | tf_op jit(solution)/shard_map/moe_outputs/pallas_call | solution.py:550
